TPU v7x, 32 devices: a whole 2x2x4 slice. The times are simulated.
32 devices in a mesh: groups: 2 (over y), aperture: 4 (over z), range: 2 (over x), beam: 2 (over core).
Axes of the slice: x: 2, y: 2, z: 4, core: 2. Of those that a mesh axis runs over, the one named last changes fastest.
Arguments:
- polar: bfloat16 [8, 256, 128, 256], P(('groups', 'range', 'beam'), 'aperture'), parts along dimension 0, may hold values from -6 to 6
- route: int32 [8, 256, 1], P(('groups', 'range', 'beam'), 'aperture'), parts along dimension 0, may hold values from 0 to 7; in each aligned block of 64 rows (0 to 63, 64 to 127, ..., all dimensions but the last counted through in order) at most 16 rows name the same one
- kind: int32 [8, 256], P(('groups', 'range', 'beam'), 'aperture'), parts along dimension 0, may hold values from 0 to 7
- filt: bfloat16 [8, 128, 256], P(('groups', 'range', 'beam')), parts along dimension 0
- interp_angle: bfloat16 [8, 128, 256], replicated
- interp_range: bfloat16 [8, 128, 256], replicated
- twiddle: float32 [8, 128], P('aperture'), may hold values from -3.140625 to 3.140625
Outputs:
- next_section: float32 [8, 8, 128, 256], P(('groups', 'range', 'beam'), 'aperture'), parts along dimension 0
There are 2 independent parts, one for each index of `groups`. A program takes and returns all parts, laid end to end along the dimension named above; an argument that names none is the same for every part. Nothing has to cross between parts.
Inputs may be any that keep to these rules, and one draw needn't show every extreme that they name: `route`: among the 64 blocks of one slab held by one device (aligned runs of 64 blocks), no tile is named more than 16 times, a bound that some block reaches.
All inputs are finite; a program needn't handle non-finite values.
Results may differ from a plain program's by a relative error of at most 0.004.
Values may be sent and summed in bfloat16 or wider, within the bound.
A program may use at most 192 MiB of HBM per device.

v0:
```python
import jax
import jax.numpy as jnp
from jax import lax
from jax.sharding import PartitionSpec as P


def swapped(value, axis, distance):
    mask = 2**distance
    pairs = [(source, source ^ mask) for source in range(lax.axis_size(axis))]
    return lax.ppermute(value, axis, pairs)


def expand(matrix):
    width = matrix.shape[-2]
    real = matrix[..., :width]
    imag = matrix[..., width:]
    top = jnp.concatenate([real, imag], axis=-1)
    bottom = jnp.concatenate([-imag, real], axis=-1)
    return jnp.concatenate([top, bottom], axis=-2)


def interpolate(comp, kinds, table_angle, table_range):
    width = comp.shape[1]
    left = table_angle[kinds]
    prod_re = jnp.einsum(
        "bij,bjk->bik", left[..., :width], comp, preferred_element_type=jnp.float32
    )
    prod_im = jnp.einsum(
        "bij,bjk->bik", left[..., width:], comp, preferred_element_type=jnp.float32
    )
    ang_re = prod_re[..., :width] - prod_im[..., width:]
    ang_im = prod_re[..., width:] + prod_im[..., :width]
    angular = jnp.concatenate([ang_re, ang_im], axis=-1).astype(jnp.bfloat16)
    right = expand(table_range[kinds])
    return jnp.einsum("bij,bjk->bik", angular, right, preferred_element_type=jnp.float32)


def per_device(polar, route, kind, filt, interp_angle, interp_range, twiddle):
    peers = lax.axis_size("aperture")
    tile_dev = twiddle.shape[0]
    tiles = tile_dev * peers
    blocks = polar[0]
    count, width, double = blocks.shape
    hmat = expand(filt[0])
    comp = jnp.dot(blocks.reshape(count * width, double), hmat, preferred_element_type=jnp.float32)
    comp = comp.reshape(count, width, double).astype(jnp.bfloat16)
    dest = route[0, :, 0]
    kinds = kind[0]
    onehot = (dest[:, None] == jnp.arange(tiles, dtype=jnp.int32)[None, :]).astype(jnp.int32)
    contrib = interpolate(comp, kinds, interp_angle, interp_range)
    partial_sum = jnp.dot(
        onehot.astype(jnp.float32).T,
        contrib.reshape(count, width * double),
        preferred_element_type=jnp.float32,
        precision=lax.Precision.HIGHEST,
    )
    partial_sum = partial_sum.reshape(tiles, width, double)
    image = lax.psum_scatter(partial_sum, "aperture", scatter_dimension=0, tiled=True)
    partner = swapped(image, "beam", 0)
    is_even = lax.axis_index("beam") == 0
    even = jnp.where(is_even, image, partner)
    odd = jnp.where(is_even, partner, image)
    sign = jnp.where(is_even, 1.0, -1.0).astype(jnp.float32)
    cos_part = jnp.cos(twiddle)[:, None, :]
    sin_part = jnp.sin(twiddle)[:, None, :]
    odd_re = odd[..., :width]
    odd_im = odd[..., width:]
    rotated = jnp.concatenate(
        [cos_part * odd_re - sin_part * odd_im, cos_part * odd_im + sin_part * odd_re], axis=-1
    )
    merged = even + sign * rotated
    return merged[None]


def solution(mesh):
    return jax.shard_map(
        per_device,
        mesh=mesh,
        in_specs=(
            P(("groups", "range", "beam"), "aperture", None, None),
            P(("groups", "range", "beam"), "aperture", None),
            P(("groups", "range", "beam"), "aperture"),
            P(("groups", "range", "beam"), None, None),
            P(),
            P(),
            P("aperture", None),
        ),
        out_specs=P(("groups", "range", "beam"), "aperture", None, None),
        check_vma=False,
    )
```

profile of v0, /device:TPU:0, one launch (start us, length us, event | category | flops | bytes accessed | tf_op | source)
XLA Modules:
  0.0 103.5 jit_solution(404142157560287981)
XLA Ops:
  6.5 0.0 copy-start
  6.5 0.0 reduce-scatter.2.cloned.1.call-start
  6.5 0.8 slice_negate_fusion.1
  7.4 5.5 %fusion = bf16[8192,256]{0,1:T(8,128)(2,1)} fusion(bf16[8192,256]{1,0:T(8,128)(2,1)} %bitcast.32, bf16[128,128]{1,0:T(8,128)(2,1)S(1)} %get-tuple-element.12, bf16[128,128]{1,0:T(8,128)(2,1)S(1)} %get-tuple-element.11, bf16[128,256]{1,0:T(8,128)(2,1)} %bitcast.34), kind=kOutput, calls=%fused_computation.3 | convolution fusion | flops 1076232192 | bytes 8519680 | tf_op jit(solution)/shard_map/dot_general | solution.py:45
  12.9 0.0 copy-start.8
  12.9 6.4 %copy.19 = bf16[8192,256]{1,0:T(8,128)(2,1)} copy(bf16[8192,256]{0,1:T(8,128)(2,1)} %fusion) | data formatting | bytes 8388608 | tf_op jit(solution)/shard_map/convert_element_type | solution.py:46
  19.3 0.0 copy-done.8
  19.3 0.0 copy-done
  19.3 2.7 %gather_fusion = bf16[64,128,256]{2,1,0:T(8,128)(2,1)} fusion(bf16[8,128,256]{2,1,0:T(8,128)(2,1)S(1)} %copy-done, s32[1024]{0:T(1024)S(1)} %pad_clamp_fusion), kind=kCustom, calls=%fused_computation | custom fusion | bytes 8388864 | tf_op jit(solution)/shard_map/gather | solution.py:24
  22.0 0.0 copy-start.1
  22.0 0.0 copy-start.4
  22.0 7.4 %fusion.15 = f32[64,128,256]{2,1,0:T(8,128)} fusion(bf16[64,128,256]{2,1,0:T(8,128)(2,1)} %bitcast.29, bf16[64,128,256]{2,1,0:T(8,128)(2,1)} %gather_fusion), kind=kOutput, calls=%fused_computation.21 | convolution fusion | flops 536870912 | bytes 14680064 | tf_op jit(solution)/shard_map/bij,bjk->bik/dot_general | solution.py:28
  29.5 0.0 copy-done.1
  29.5 0.0 copy-done.4
  29.5 4.5 %fusion.17 = f32[64,128,256]{2,1,0:T(8,128)} fusion(bf16[64,128,256]{2,1,0:T(8,128)(2,1)S(1)} %bitcast.30, bf16[64,128,256]{2,1,0:T(8,128)(2,1)S(1)} %copy-done.4), kind=kOutput, calls=%fused_computation.23 | convolution fusion | flops 536870912 | bytes 14680064 | tf_op jit(solution)/shard_map/bij,bjk->bik/dot_general | solution.py:25
  33.9 0.0 copy-done.3
  34.0 2.8 %gather_fusion.1 = bf16[64,128,256]{2,1,0:T(8,128)(2,1)} fusion(bf16[8,128,256]{2,1,0:T(8,128)(2,1)S(1)} %copy-done.3, s32[1024]{0:T(1024)S(1)} %pad_clamp_fusion), kind=kCustom, calls=%fused_computation.1 | custom fusion | bytes 8388864 | tf_op jit(solution)/shard_map/gather | solution.py:34
  36.7 4.9 %slice_negate_fusion = (bf16[64,128,128]{2,1,0:T(8,128)(2,1)}, bf16[64,128,128]{2,1,0:T(8,128)(2,1)}) fusion(bf16[64,128,256]{2,1,0:T(8,128)(2,1)} %gather_fusion.1), kind=kLoop, calls=%fused_computation.20 | loop fusion | flops 1048576 | bytes 8388608 | tf_op jit(solution)/shard_map/neg | solution.py:18
  41.6 1.2 %copy-done.2 = f32[64,128,256]{2,1,0:T(8,128)S(1)} copy-done((f32[64,128,256]{2,1,0:T(8,128)S(1)}, f32[64,128,256]{2,1,0:T(8,128)}, u32[]{:S(2)}) %copy-start.2) | copy-done | bytes 8388632
  42.9 5.7 %fusion.11 = (bf16[64,128,128]{2,1,0:T(8,128)(2,1)}, bf16[64,128,128]{2,1,0:T(8,128)(2,1)}) fusion(f32[64,128,256]{2,1,0:T(8,128)S(1)} %copy-done.2, f32[64,128,256]{2,1,0:T(8,128)} %fusion.17), kind=kLoop, calls=%fused_computation.16 | loop fusion | flops 4194304 | bytes 20971520 | tf_op jit(solution)/shard_map/convert
  48.6 0.0 copy-done.5
  48.6 4.5 %fusion.4 = f32[64,128,256]{2,1,0:T(8,128)S(1)} fusion(bf16[64,128,128]{2,1,0:T(8,128)(2,1)} %get-tuple-element.8, bf16[64,128,128]{2,1,0:T(8,128)(2,1)} %get-tuple-element.7, bf16[64,128,256]{2,1,0:T(8,128)(2,1)S(1)} %copy-done.5, bf16[64,128,128]{2,1,0:T(8,128)(2,1)} %get-tuple-element.6, bf16[64,128,128]{2,1,0:T(8,128)(2,1)} %get-tuple-element.5), kind=kOutput, calls=%fused_computation.7 | convolution fusion | flops 1107296256 | bytes 20971520 | tf_op jit(solution)/shard_map/bij,bjk->bik/dot_general | solution.py:35
  53.1 0.0 copy-done.7
  53.1 0.0 copy-start.6
  53.2 8.6 %fusion.1 = f32[8,128,256]{2,0,1:T(8,128)S(1)} fusion(s32[64]{0:T(128)S(1)} %bitcast.35, f32[8,8,128,256]{3,2,1,0:T(8,128)S(1)} %bitcast.31), kind=kOutput, calls=%fused_computation.4 | convolution fusion | flops 201328128 | bytes 9437440 | tf_op jit(solution)/shard_map/dot_general | solution.py:51
  61.8 1.3 %copy.18 = f32[8,128,256]{2,1,0:T(8,128)} copy(f32[8,128,256]{2,0,1:T(8,128)S(1)} %fusion.1) | data formatting | bytes 2097152 | tf_op jit(solution)/shard_map/dot_general | solution.py:51
  63.1 0.0 reduce-scatter.2.cloned.1.call-update
  63.1 30.0 %reduce-scatter.2.cloned.1.call-done = f32[2,128,256]{2,1,0:T(8,128)} async-done(((f32[8,128,256]{2,1,0:T(8,128)}), f32[2,128,256]{2,1,0:T(8,128)}) %reduce-scatter.2.cloned.1.call-update) | async-done | bytes 262160 | tf_op jit(solution)/shard_map/reduce_scatter | solution.py:58
  93.1 0.0 collective-permute-start
  93.1 0.0 copy-done.6
  93.1 1.7 %collective-permute-done = f32[2,128,256]{2,1,0:T(8,128)S(1)} collective-permute-done((f32[2,128,256]{2,1,0:T(8,128)}, f32[2,128,256]{2,1,0:T(8,128)S(1)}, u32[]{:S(2)}, u32[]{:S(2)}) %collective-permute-start) | collective-permute-done | bytes 262176 | tf_op jit(solution)/shard_map/ppermute | solution.py:10
  94.9 1.7 %fusion.20 = f32[1,2,128,256]{3,2,1,0:T(8,128)} fusion(f32[2,128,128]{2,1,0:T(8,128)S(1)} %get-tuple-element.10, f32[2,128,128]{2,1,0:T(8,128)S(1)} %get-tuple-element.9, f32[2,128,256]{2,1,0:T(8,128)} %reduce-scatter.2.cloned.1.call-done, f32[2,128,256]{2,1,0:T(8,128)S(1)} %collective-permute-done, f32[]{:T(128)S(6)} %select_n.30, pred[]{:T(512)S(6)} %eq.18), kind=kLoop, calls=%fused_computation.27 | loop fusion | flops 262144 | bytes 1048581 | tf_op jit(solution)/shard_map/broadcast_in_dim | solution.py:72
  (9 shorter events, 0.1 us)
Async XLA Ops:
  6.5 12.8 %copy-start = (bf16[8,128,256]{2,1,0:T(8,128)(2,1)S(1)}, bf16[8,128,256]{2,1,0:T(8,128)(2,1)}, u32[]{:S(2)}) copy-start(bf16[8,128,256]{2,1,0:T(8,128)(2,1)} %param.11) | copy-start | bytes 1572868
  6.5 86.6 %reduce-scatter.2.cloned.1.call-start = ((), (), s32[]{:S(2)}) async-start(), calls=%async_computation.1 | async-start | bytes 1310720 | tf_op jit(solution)/shard_map/reduce_scatter | solution.py:58
  12.9 6.4 %copy-start.8 = (s32[1,64]{1,0:T(1,128)S(1)}, s32[1,64]{1,0:T(1,128)}, u32[]{:S(2)}) copy-start(s32[1,64]{1,0:T(1,128)} %param.9) | copy-start | bytes 772
  22.0 7.4 %copy-start.1 = (bf16[8192,256]{1,0:T(8,128)(2,1)S(1)}, bf16[8192,256]{1,0:T(8,128)(2,1)}, u32[]{:S(2)}) copy-start(bf16[8192,256]{1,0:T(8,128)(2,1)} %copy.19) | copy-start | bytes 12582916
  22.0 7.4 %copy-start.4 = (bf16[64,128,256]{2,1,0:T(8,128)(2,1)S(1)}, bf16[64,128,256]{2,1,0:T(8,128)(2,1)}, u32[]{:S(2)}) copy-start(bf16[64,128,256]{2,1,0:T(8,128)(2,1)} %gather_fusion) | copy-start | bytes 12582916
  29.5 4.5 %copy-start.3 = (bf16[8,128,256]{2,1,0:T(8,128)(2,1)S(1)}, bf16[8,128,256]{2,1,0:T(8,128)(2,1)}, u32[]{:S(2)}) copy-start(bf16[8,128,256]{2,1,0:T(8,128)(2,1)} %param.12) | copy-start | bytes 1572868
  36.7 6.2 %copy-start.2 = (f32[64,128,256]{2,1,0:T(8,128)S(1)}, f32[64,128,256]{2,1,0:T(8,128)}, u32[]{:S(2)}) copy-start(f32[64,128,256]{2,1,0:T(8,128)} %fusion.15) | copy-start | bytes 25165828
  42.9 5.7 %copy-start.5 = (bf16[64,128,256]{2,1,0:T(8,128)(2,1)S(1)}, bf16[64,128,256]{2,1,0:T(8,128)(2,1)}, u32[]{:S(2)}) copy-start(bf16[64,128,256]{2,1,0:T(8,128)(2,1)} %gather_fusion.1) | copy-start | bytes 12582916
  48.6 4.5 %copy-start.7 = (s32[1,64,1]{1,2,0:T(1,128)S(1)}, s32[1,64,1]{1,2,0:T(1,128)}, u32[]{:S(2)}) copy-start(s32[1,64,1]{1,2,0:T(1,128)} %param.8) | copy-start | bytes 772
  53.1 40.0 %copy-start.6 = (f32[2,128]{1,0:T(2,128)S(1)}, f32[2,128]{1,0:T(2,128)}, u32[]{:S(2)}) copy-start(f32[2,128]{1,0:T(2,128)} %param.13) | copy-start | bytes 3076
  93.1 1.7 %collective-permute-start = (f32[2,128,256]{2,1,0:T(8,128)}, f32[2,128,256]{2,1,0:T(8,128)S(1)}, u32[]{:S(2)}, u32[]{:S(2)}) collective-permute-start(f32[2,128,256]{2,1,0:T(8,128)} %reduce-scatter.2.cloned.1.call-done), channel_id=1, source_target_pairs={{0,1},{1,0},{2,3},{3,2},{4,5},{5,4},{6,7},{7,6},{8,9},{9,8},{10,11... | collective-permute-start | bytes 786440 | tf_op jit(solution)/shard_map/ppermute | solution.py:10
Sparse Core Ops, SparseCore 0:
  63.2 29.8 reduce-scatter.1
where the time goes:
time: 104 us; the launch traced here: 103 us
  waiting for transfers between devices  31.7 us (30%)
  matrix products  30.5 us (29%)
  local copies, waits for them, and re-layouts  14.5 us (14%)
  between operations  13.5 us (13%)
  other arithmetic  13.3 us (13%)
    reduce_scatter x1, waiting for transfers between devices, per_device(): lax.psum_scatter(partial_sum, 'aperture', scatter_dimension=0, tiled=True)  30 us
    dot_general x1, matrix products, per_device(): jnp.dot(onehot.astype(jnp.float32).T, contrib.reshape(count, width * doub...  8.62 us
    dot_general x1, matrix products, interpolate(): jnp.einsum('bij,bjk->bik', left[..., width:], comp, preferred_element_typ...  7.42 us
    convert_element_type x1, local copies, waits for them, and re-layouts, per_device(): comp = comp.reshape(count, width, double).astype(jnp.bfloat16)  6.39 us
    neg x2, other arithmetic, expand(): bottom = jnp.concatenate([-imag, real], axis=-1)  5.75 us
    another operation x1, other arithmetic  5.73 us
    dot_general x1, matrix products, per_device(): jnp.dot(blocks.reshape(count * width, double), hmat, preferred_element_ty...  5.5 us
    dot_general x1, matrix products, interpolate(): jnp.einsum('bij,bjk->bik', angular, right, preferred_element_type=jnp.flo...  4.51 us
  transfers between devices with their start and end apart: 2, of which 2 were waited for; matrix products, arithmetic and copies ran while one was open for 0% of the time, Pallas kernels for 0%

commit v1 on v0

v1 whole, which is shorter than its diff:
```python
import functools

import jax
import jax.numpy as jnp
from jax import lax
from jax.experimental import pallas as pl
from jax.experimental.pallas import tpu as pltpu
from jax.sharding import PartitionSpec as P

MESH = pl.DeviceIdType.MESH
CHUNKS = 8
PIECES = 4
GROUP = 2


def expand(matrix, width):
    real, imag = matrix[:, :width], matrix[:, width:]
    return jnp.concatenate(
        [jnp.concatenate([real, imag], axis=1), jnp.concatenate([-imag, real], axis=1)], axis=0
    )


def angle_kernel(
    nkern, route, kind, filt_hbm, angle_hbm, rng_hbm, polar, y, ghi, glo,
    filt, angle, rng, pbuf, table_sems, sems
):
    count, width, double = pbuf.shape
    per = count // CHUNKS

    def chunk_copy(c):
        part = pl.ds(c * per, per)
        return pltpu.make_async_copy(polar.at[part], pbuf.at[part], sems.at[c])

    tables = [
        pltpu.make_async_copy(src, dst, table_sems.at[i])
        for i, (src, dst) in enumerate(((filt_hbm, filt), (rng_hbm, rng), (angle_hbm, angle)))
    ]
    for copy in tables:
        copy.start()
    for c in range(CHUNKS):
        chunk_copy(c).start()

    @pl.loop(0, y.shape[0])
    def _(cell):
        y[cell] = jnp.zeros((width, double), jnp.float32)

    tables[0].wait()
    tables[1].wait()

    @pl.loop(0, nkern)
    def _(k):
        g = jnp.dot(filt[...], expand(rng[k], width), preferred_element_type=jnp.float32)
        hi = g.astype(jnp.bfloat16)
        lo = (g - hi.astype(jnp.float32)).astype(jnp.bfloat16)
        rows = pl.ds(pl.multiple_of(k * double, double), double)
        ghi[rows, :] = expand(hi, width)
        glo[rows, :] = expand(lo, width)

    tables[2].wait()

    @pl.loop(0, CHUNKS)
    def _(c):
        chunk_copy(c).wait()

        @pl.loop(0, per // GROUP)
        def _(g):
            outs = []
            cells = []
            for u in range(GROUP):
                j = c * per + g * GROUP + u
                k = kind[j]
                cells.append(route[j] * nkern + k)
                outs.append(
                    jnp.dot(
                        angle[k], expand(pbuf[j], width), preferred_element_type=jnp.float32
                    )
                )
            for cell, out in zip(cells, outs):
                y[cell] += out


def merge_kernel(
    n, y, ghi, glo, twiddle, out, xcat, own, sbuf, rbuf_r, rbuf_l, pair,
    send_sem, recv_r, recv_l, pair_send, pair_recv,
):
    tile_dev, width, double = out.shape
    rows = tile_dev * width
    nkern = ghi.shape[0] // double
    piece = rows // PIECES
    z = lax.axis_index("aperture")
    b = lax.axis_index("beam")
    has_left = z > 0
    has_right = z < n - 1

    barrier = pltpu.get_barrier_semaphore()

    @pl.when(has_left)
    def _():
        pl.semaphore_signal(barrier, inc=1, device_id={"aperture": z - 1}, device_id_type=MESH)

    @pl.when(has_right)
    def _():
        pl.semaphore_signal(barrier, inc=1, device_id={"aperture": z + 1}, device_id_type=MESH)

    pl.semaphore_signal(barrier, inc=1, device_id={"beam": 1 - b}, device_id_type=MESH)

    ahead = n - 1 - z
    near = jnp.minimum(ahead, z)
    lead = jnp.maximum(ahead, z) - near

    def dest(i):
        first = jnp.where(ahead > z, n - 1 - i, i)
        j = i - lead
        gap = near - j // 2
        later = jnp.where(j % 2 == 0, z + gap, z - gap)
        return jnp.where(i < lead, first, later)

    def span(p):
        return pl.ds(p * piece, piece)

    def send_right(d, p):
        return pltpu.make_async_remote_copy(
            src_ref=sbuf.at[d, span(p)], dst_ref=rbuf_r.at[d, span(p)],
            send_sem=send_sem.at[d, p], recv_sem=recv_r.at[d, p],
            device_id={"aperture": z + 1}, device_id_type=MESH,
        )

    def send_left(d, p):
        return pltpu.make_async_remote_copy(
            src_ref=sbuf.at[d, span(p)], dst_ref=rbuf_l.at[d, span(p)],
            send_sem=send_sem.at[d, p], recv_sem=recv_l.at[d, p],
            device_id={"aperture": z - 1}, device_id_type=MESH,
        )

    def send_pair(p):
        return pltpu.make_async_remote_copy(
            src_ref=own.at[z, span(p)], dst_ref=pair.at[span(p)],
            send_sem=pair_send.at[p], recv_sem=pair_recv.at[p],
            device_id={"beam": 1 - b}, device_id_type=MESH,
        )

    @pl.loop(0, n)
    def _(i):
        d = dest(i)
        for t in range(tile_dev):
            for k in range(nkern):
                xcat[t * width:(t + 1) * width, k * double:(k + 1) * double] = y[
                    (d * tile_dev + t) * nkern + k
                ].astype(jnp.bfloat16)
        own[d] = jnp.dot(xcat[...], ghi[...], preferred_element_type=jnp.float32) + jnp.dot(
            xcat[...], glo[...], preferred_element_type=jnp.float32
        )

        @pl.when(i == 0)
        def _():
            links = has_left.astype(jnp.int32) + has_right.astype(jnp.int32) + 1
            pl.semaphore_wait(barrier, links)

        @pl.when(jnp.logical_and(z == 0, d > z))
        def _():
            sbuf[d] = own[d].astype(jnp.bfloat16)
            for p in range(PIECES):
                send_right(d, p).start()

        @pl.when(jnp.logical_and(z == n - 1, d < z))
        def _():
            sbuf[d] = own[d].astype(jnp.bfloat16)
            for p in range(PIECES):
                send_left(d, p).start()

    @pl.when(jnp.logical_and(has_left, has_right))
    def _():
        @pl.loop(0, n - 1)
        def _(i):
            d = dest(i)

            @pl.when(d > z)
            def _():
                for p in range(PIECES):
                    send_right(d, p).wait_recv()
                    part = own[d, span(p)] + rbuf_r[d, span(p)].astype(jnp.float32)
                    sbuf[d, span(p)] = part.astype(jnp.bfloat16)
                    send_right(d, p).start()

            @pl.when(d < z)
            def _():
                for p in range(PIECES):
                    send_left(d, p).wait_recv()
                    part = own[d, span(p)] + rbuf_l[d, span(p)].astype(jnp.float32)
                    sbuf[d, span(p)] = part.astype(jnp.bfloat16)
                    send_left(d, p).start()

    for p in range(PIECES):
        @pl.when(has_left)
        def _():
            send_right(z, p).wait_recv()
            own[z, span(p)] += rbuf_r[z, span(p)].astype(jnp.float32)

        @pl.when(has_right)
        def _():
            send_left(z, p).wait_recv()
            own[z, span(p)] += rbuf_l[z, span(p)].astype(jnp.float32)

        send_pair(p).start()

    cos_all, sin_all = jnp.cos(twiddle[...]), jnp.sin(twiddle[...])
    is_even = b == 0
    sign = jnp.where(is_even, 1.0, -1.0).astype(jnp.float32)
    for p in range(PIECES):
        send_pair(p).wait_recv()
        t, base = p * piece // width, p * piece % width
        mine, other = own[z, span(p)], pair[span(p)]
        even = jnp.where(is_even, mine, other)
        odd = jnp.where(is_even, other, mine)
        cos, sin = cos_all[t:t + 1], sin_all[t:t + 1]
        odd_re, odd_im = odd[:, :width], odd[:, width:]
        out[t, base:base + piece, :width] = even[:, :width] + sign * (cos * odd_re - sin * odd_im)
        out[t, base:base + piece, width:] = even[:, width:] + sign * (cos * odd_im + sin * odd_re)

    for p in range(PIECES):
        send_pair(p).wait_send()

    @pl.loop(0, n)
    def _(d):
        @pl.when(d != z)
        def _():
            for p in range(PIECES):
                send_right(d, p).wait_send()


def per_device(polar, route, kind, filt, interp_angle, interp_range, twiddle):
    n = lax.axis_size("aperture")
    tile_dev = twiddle.shape[0]
    tiles = tile_dev * n
    _, count, width, double = polar.shape
    nkern = interp_angle.shape[0]
    cells = tiles * nkern
    rows = tile_dev * width
    resident = cells * width * double * 4 <= 16 * 2**20
    held = pltpu.VMEM if resident else jax.ShapeDtypeStruct
    vmem = pl.BlockSpec(memory_space=pltpu.VMEM)
    smem = pl.BlockSpec(memory_space=pltpu.SMEM)
    y, ghi, glo = pl.pallas_call(
        functools.partial(angle_kernel, nkern),
        out_shape=[
            held((cells, width, double), jnp.float32),
            held((nkern * double, double), jnp.bfloat16),
            held((nkern * double, double), jnp.bfloat16),
        ],
        in_specs=[smem, smem] + [pl.BlockSpec(memory_space=pl.ANY)] * 4,
        out_specs=[vmem, vmem, vmem],
        scratch_shapes=[
            pltpu.VMEM((width, double), jnp.bfloat16),
            pltpu.VMEM((nkern, width, double), jnp.bfloat16),
            pltpu.VMEM((nkern, width, double), jnp.bfloat16),
            pltpu.VMEM((count, width, double), jnp.bfloat16),
            pltpu.SemaphoreType.DMA((3,)),
            pltpu.SemaphoreType.DMA((CHUNKS,)),
        ],
        compiler_params=pltpu.CompilerParams(vmem_limit_bytes=(24 if resident else 48) * 2**20),
        name="angle",
    )(
        *[
            pltpu.with_memory_space_constraint(v, pltpu.HBM)
            for v in (route[0, :, 0], kind[0], filt[0], interp_angle, interp_range, polar[0])
        ],
    )
    if resident:
        y, ghi, glo = [pltpu.with_memory_space_constraint(v, pltpu.VMEM) for v in (y, ghi, glo)]
    merged = pl.pallas_call(
        functools.partial(merge_kernel, n),
        out_shape=jax.ShapeDtypeStruct((tile_dev, width, double), jnp.float32),
        in_specs=[vmem, vmem, vmem, vmem],
        out_specs=vmem,
        scratch_shapes=[
            pltpu.VMEM((rows, nkern * double), jnp.bfloat16),
            pltpu.VMEM((n, rows, double), jnp.float32),
            pltpu.VMEM((n, rows, double), jnp.bfloat16),
            pltpu.VMEM((n, rows, double), jnp.bfloat16),
            pltpu.VMEM((n, rows, double), jnp.bfloat16),
            pltpu.VMEM((rows, double), jnp.float32),
            pltpu.SemaphoreType.DMA((n, PIECES)),
            pltpu.SemaphoreType.DMA((n, PIECES)),
            pltpu.SemaphoreType.DMA((n, PIECES)),
            pltpu.SemaphoreType.DMA((PIECES,)),
            pltpu.SemaphoreType.DMA((PIECES,)),
        ],
        compiler_params=pltpu.CompilerParams(
            vmem_limit_bytes=(24 if resident else 58) * 2**20, collective_id=0, has_side_effects=True
        ),
        name="merge",
    )(y, ghi, glo, pltpu.with_memory_space_constraint(twiddle, pltpu.HBM))
    return merged[None]


def solution(mesh):
    return jax.shard_map(
        per_device,
        mesh=mesh,
        in_specs=(
            P(("groups", "range", "beam"), "aperture", None, None),
            P(("groups", "range", "beam"), "aperture", None),
            P(("groups", "range", "beam"), "aperture"),
            P(("groups", "range", "beam"), None, None),
            P(),
            P(),
            P("aperture", None),
        ),
        out_specs=P(("groups", "range", "beam"), "aperture", None, None),
        check_vma=False,
    )
```

time: 104 us -> 29.2 us (0.28)
  waiting for transfers between devices: 31.7 us -> 0 us
  matrix products: 30.5 us -> 0 us
  Pallas kernels: 0 us -> 28.3 us
  local copies, waits for them, and re-layouts: 14.5 us -> 0.71 us
  between operations: 13.5 us -> 0.02 us
  other arithmetic: 13.3 us -> 0 us
    dot_general x5 -> x0, matrix products: 30.5 us -> none  [the longest x1 8.62 us: per_device(): jnp.dot(onehot.astype(jnp.float32).T, contrib.reshape(count, width * doub...]
    reduce_scatter x1 -> x0, waiting for transfers between devices: 30 us -> none  [per_device(): lax.psum_scatter(partial_sum, 'aperture', scatter_dimension=0, tiled=True)]
    pallas_call x0 -> x2, Pallas kernels: none -> 28.3 us  [the longest x1 17.5 us: per_device(): pl.pallas_call(functools.partial(merge_kernel, n), out_shape=jax.ShapeDty...]
    convert_element_type x1 -> x0, local copies, waits for them, and re-layouts: 6.39 us -> none  [per_device(): comp = comp.reshape(count, width, double).astype(jnp.bfloat16)]
    neg x2 -> x0, other arithmetic: 5.75 us -> none  [expand(): bottom = jnp.concatenate([-imag, real], axis=-1)]
    another operation x1 -> x0, other arithmetic: 5.73 us -> none
    gather x2 -> x0, local copies, waits for them, and re-layouts: 5.5 us -> none  [the longest x1 2.76 us: interpolate(): right = expand(table_range[kinds])]
    broadcast_in_dim x1 -> x0, other arithmetic: 1.72 us -> none  [per_device(): return merged[None]]
  transfers between devices with their start and end apart: 2 -> 0, of which waited for: 2 -> 0; matrix products, arithmetic and copies ran while one was open for 0% -> 0% of each run, Pallas kernels for 0% -> 0%
where the time goes in v1:
time: 29.2 us; the launch traced here: 29 us
  Pallas kernels  28.3 us (97%)
  local copies, waits for them, and re-layouts  0.71 us (2%)
    pallas_call x1, Pallas kernels, per_device(): pl.pallas_call(functools.partial(merge_kernel, n), out_shape=jax.ShapeDty...  17.5 us
    pallas_call x1, Pallas kernels, per_device(): pl.pallas_call(functools.partial(angle_kernel, nkern), out_shape=[held((c...  10.8 us
    unnamed x1, local copies, waits for them, and re-layouts  0.71 us

profile of v1, /device:TPU:0, one launch (start us, length us, event | category | flops | bytes accessed | tf_op | source)
XLA Modules:
  0.0 29.0 jit_solution(8848625123938781294)
XLA Ops:
  0.0 10.8 %angle.1 = (f32[64,128,256]{2,1,0:T(8,128)S(1)}, bf16[2048,256]{1,0:T(8,128)(2,1)S(1)}, bf16[2048,256]{1,0:T(8,128)(2,1)S(1)}) custom-call(s32[64]{0:T(128)} %bitcast.8, s32[64]{0:T(128)} %bitcast.9, bf16[128,256]{1,0:T(8,128)(2,1)} %bitcast.7, bf16[8,128,256]{2,1,0:T(8,128)(2,1)} %angle_hbm.1, bf16[8,128,256]{2,1,0:T(8,128)(2,1)} %rng_hbm.1, ...), custom_call_target="tpu_custom_call" | custom-call | tf_op jit(solution)/shard_map/angle/pallas_call | solution.py:243
  10.8 17.5 %merge.1 = f32[2,128,256]{2,1,0:T(8,128)S(1)} custom-call(f32[64,128,256]{2,1,0:T(8,128)S(1)} %get-tuple-element.8.y, bf16[2048,256]{1,0:T(8,128)(2,1)S(1)} %get-tuple-element.9.ghi, bf16[2048,256]{1,0:T(8,128)(2,1)S(1)} %get-tuple-element.10.glo, f32[2,128]{1,0:T(2,128)} %twiddle.1), custom_call_target="tpu_custom_call" | custom-call | tf_op jit(solution)/shard_map/merge/pallas_call | solution.py:270
  28.3 0.7 %copy.9 = f32[1,2,128,256]{3,2,1,0:T(8,128)} copy(f32[1,2,128,256]{3,2,1,0:T(8,128)S(1)} %bitcast.5) | data formatting | bytes 524288

commit v2 on v1

--- a/solution.py
+++ b/solution.py
@@ -8,9 +8,8 @@
 from jax.sharding import PartitionSpec as P
 
 MESH = pl.DeviceIdType.MESH
-CHUNKS = 8
-PIECES = 4
-GROUP = 2
+CHUNKS = 2
+PIECES = 8
 
 
 def expand(matrix, width):
@@ -40,21 +39,21 @@
     for c in range(CHUNKS):
         chunk_copy(c).start()
 
-    @pl.loop(0, y.shape[0])
-    def _(cell):
-        y[cell] = jnp.zeros((width, double), jnp.float32)
-
     tables[0].wait()
     tables[1].wait()
 
-    @pl.loop(0, nkern)
-    def _(k):
-        g = jnp.dot(filt[...], expand(rng[k], width), preferred_element_type=jnp.float32)
+    products = [
+        jnp.dot(filt[...], expand(rng[k], width), preferred_element_type=jnp.float32)
+        for k in range(nkern)
+    ]
+    share = y.shape[0] // nkern
+    for k, g in enumerate(products):
+        for cell in range(k * share, (k + 1) * share):
+            y[cell] = jnp.zeros((width, double), jnp.float32)
         hi = g.astype(jnp.bfloat16)
         lo = (g - hi.astype(jnp.float32)).astype(jnp.bfloat16)
-        rows = pl.ds(pl.multiple_of(k * double, double), double)
-        ghi[rows, :] = expand(hi, width)
-        glo[rows, :] = expand(lo, width)
+        ghi[k * double:(k + 1) * double, :] = expand(hi, width)
+        glo[k * double:(k + 1) * double, :] = expand(lo, width)
 
     tables[2].wait()
 
@@ -62,21 +61,17 @@
     def _(c):
         chunk_copy(c).wait()
 
-        @pl.loop(0, per // GROUP)
-        def _(g):
-            outs = []
-            cells = []
-            for u in range(GROUP):
-                j = c * per + g * GROUP + u
-                k = kind[j]
-                cells.append(route[j] * nkern + k)
-                outs.append(
-                    jnp.dot(
-                        angle[k], expand(pbuf[j], width), preferred_element_type=jnp.float32
-                    )
-                )
-            for cell, out in zip(cells, outs):
-                y[cell] += out
+        outs = []
+        cells = []
+        for u in range(per):
+            j = c * per + u
+            k = kind[j]
+            cells.append(route[j] * nkern + k)
+            outs.append(
+                jnp.dot(angle[k], expand(pbuf[j], width), preferred_element_type=jnp.float32)
+            )
+        for cell, out in zip(cells, outs):
+            y[cell] += out
 
 
 def merge_kernel(

time: 29.2 us -> 23 us (0.79)
  Pallas kernels: 28.3 us -> 22.1 us
    pallas_call x1, Pallas kernels: 10.8 us -> 4.31 us  [per_device(): pl.pallas_call(functools.partial(angle_kernel, nkern), out_shape=[held((c...]
where the time goes in v2:
time: 23 us; the launch traced here: 22.8 us
  Pallas kernels  22.1 us (96%)
  local copies, waits for them, and re-layouts  0.71 us (3%)
    pallas_call x1, Pallas kernels, per_device(): pl.pallas_call(functools.partial(merge_kernel, n), out_shape=jax.ShapeDty...  17.8 us
    pallas_call x1, Pallas kernels, per_device(): pl.pallas_call(functools.partial(angle_kernel, nkern), out_shape=[held((c...  4.31 us
    unnamed x1, local copies, waits for them, and re-layouts  0.71 us

profile of v2, /device:TPU:0, one launch (start us, length us, event | category | flops | bytes accessed | tf_op | source)
XLA Modules:
  0.0 22.8 jit_solution(2687509394140538700)
XLA Ops:
  0.0 4.3 %angle.1 = (f32[64,128,256]{2,1,0:T(8,128)S(1)}, bf16[2048,256]{1,0:T(8,128)(2,1)S(1)}, bf16[2048,256]{1,0:T(8,128)(2,1)S(1)}) custom-call(s32[64]{0:T(128)} %bitcast.8, s32[64]{0:T(128)} %bitcast.9, bf16[128,256]{1,0:T(8,128)(2,1)} %bitcast.7, bf16[8,128,256]{2,1,0:T(8,128)(2,1)} %angle_hbm.1, bf16[8,128,256]{2,1,0:T(8,128)(2,1)} %rng_hbm.1, ...), custom_call_target="tpu_custom_call" | custom-call | tf_op jit(solution)/shard_map/angle/pallas_call | solution.py:238
  4.3 17.8 %merge.1 = f32[2,128,256]{2,1,0:T(8,128)S(1)} custom-call(f32[64,128,256]{2,1,0:T(8,128)S(1)} %get-tuple-element.8.y, bf16[2048,256]{1,0:T(8,128)(2,1)S(1)} %get-tuple-element.9.ghi, bf16[2048,256]{1,0:T(8,128)(2,1)S(1)} %get-tuple-element.10.glo, f32[2,128]{1,0:T(2,128)} %twiddle.1), custom_call_target="tpu_custom_call" | custom-call | tf_op jit(solution)/shard_map/merge/pallas_call | solution.py:265
  22.1 0.7 %copy.9 = f32[1,2,128,256]{3,2,1,0:T(8,128)} copy(f32[1,2,128,256]{3,2,1,0:T(8,128)S(1)} %bitcast.5) | data formatting | bytes 524288

commit v3 on v2

--- a/solution.py
+++ b/solution.py
@@ -9,7 +9,7 @@
 
 MESH = pl.DeviceIdType.MESH
 CHUNKS = 2
-PIECES = 8
+PIECES = 4
 
 
 def expand(matrix, width):
@@ -165,25 +165,46 @@
 
     @pl.when(jnp.logical_and(has_left, has_right))
     def _():
+        def pass_right(d, p):
+            send_right(d, p).wait_recv()
+            part = own[d, span(p)] + rbuf_r[d, span(p)].astype(jnp.float32)
+            sbuf[d, span(p)] = part.astype(jnp.bfloat16)
+            send_right(d, p).start()
+
+        def pass_left(d, p):
+            send_left(d, p).wait_recv()
+            part = own[d, span(p)] + rbuf_l[d, span(p)].astype(jnp.float32)
+            sbuf[d, span(p)] = part.astype(jnp.bfloat16)
+            send_left(d, p).start()
+
         @pl.loop(0, n - 1)
         def _(i):
-            d = dest(i)
-
-            @pl.when(d > z)
+            @pl.when(jnp.logical_and(i < lead, ahead > z))
             def _():
                 for p in range(PIECES):
-                    send_right(d, p).wait_recv()
-                    part = own[d, span(p)] + rbuf_r[d, span(p)].astype(jnp.float32)
-                    sbuf[d, span(p)] = part.astype(jnp.bfloat16)
-                    send_right(d, p).start()
-
-            @pl.when(d < z)
+                    pass_right(n - 1 - i, p)
+
+            @pl.when(jnp.logical_and(i < lead, ahead < z))
             def _():
                 for p in range(PIECES):
-                    send_left(d, p).wait_recv()
-                    part = own[d, span(p)] + rbuf_l[d, span(p)].astype(jnp.float32)
-                    sbuf[d, span(p)] = part.astype(jnp.bfloat16)
-                    send_left(d, p).start()
+                    pass_left(i, p)
+
+        @pl.loop(0, n // 2)
+        def _(i):
+            gap = near - i
+
+            @pl.when(i < near)
+            def _():
+                for p in range(PIECES):
+                    @pl.when(ahead > z)
+                    def _():
+                        pass_right(z + gap, p)
+
+                    pass_left(z - gap, p)
+
+                    @pl.when(ahead <= z)
+                    def _():
+                        pass_right(z + gap, p)
 
     for p in range(PIECES):
         @pl.when(has_left)

time: 23 us -> 22.5 us (0.978)
  Pallas kernels: 22.1 us -> 21.7 us
    pallas_call x1, Pallas kernels: 17.8 us -> 17.3 us  [per_device(): pl.pallas_call(functools.partial(merge_kernel, n), out_shape=jax.ShapeDty...]
where the time goes in v3:
time: 22.5 us; the launch traced here: 22.4 us
  Pallas kernels  21.7 us (96%)
  local copies, waits for them, and re-layouts  0.71 us (3%)
    pallas_call x1, Pallas kernels, per_device(): pl.pallas_call(functools.partial(merge_kernel, n), out_shape=jax.ShapeDty...  17.3 us
    pallas_call x1, Pallas kernels, per_device(): pl.pallas_call(functools.partial(angle_kernel, nkern), out_shape=[held((c...  4.31 us
    unnamed x1, local copies, waits for them, and re-layouts  0.71 us

profile of v3, /device:TPU:0, one launch (start us, length us, event | category | flops | bytes accessed | tf_op | source)
XLA Modules:
  0.0 22.4 jit_solution(2385997438896259420)
XLA Ops:
  0.0 4.3 %angle.1 = (f32[64,128,256]{2,1,0:T(8,128)S(1)}, bf16[2048,256]{1,0:T(8,128)(2,1)S(1)}, bf16[2048,256]{1,0:T(8,128)(2,1)S(1)}) custom-call(s32[64]{0:T(128)} %bitcast.8, s32[64]{0:T(128)} %bitcast.9, bf16[128,256]{1,0:T(8,128)(2,1)} %bitcast.7, bf16[8,128,256]{2,1,0:T(8,128)(2,1)} %angle_hbm.1, bf16[8,128,256]{2,1,0:T(8,128)(2,1)} %rng_hbm.1, ...), custom_call_target="tpu_custom_call" | custom-call | tf_op jit(solution)/shard_map/angle/pallas_call | solution.py:259
  4.3 17.3 %merge.1 = f32[2,128,256]{2,1,0:T(8,128)S(1)} custom-call(f32[64,128,256]{2,1,0:T(8,128)S(1)} %get-tuple-element.8.y, bf16[2048,256]{1,0:T(8,128)(2,1)S(1)} %get-tuple-element.9.ghi, bf16[2048,256]{1,0:T(8,128)(2,1)S(1)} %get-tuple-element.10.glo, f32[2,128]{1,0:T(2,128)} %twiddle.1), custom_call_target="tpu_custom_call" | custom-call | tf_op jit(solution)/shard_map/merge/pallas_call | solution.py:286
  21.7 0.7 %copy.9 = f32[1,2,128,256]{3,2,1,0:T(8,128)} copy(f32[1,2,128,256]{3,2,1,0:T(8,128)S(1)} %bitcast.5) | data formatting | bytes 524288

commit v4 on v3

--- a/solution.py
+++ b/solution.py
@@ -134,9 +134,7 @@
             device_id={"beam": 1 - b}, device_id_type=MESH,
         )
 
-    @pl.loop(0, n)
-    def _(i):
-        d = dest(i)
+    def gather_item(d):
         for t in range(tile_dev):
             for k in range(nkern):
                 xcat[t * width:(t + 1) * width, k * double:(k + 1) * double] = y[
@@ -146,6 +144,11 @@
             xcat[...], glo[...], preferred_element_type=jnp.float32
         )
 
+    @pl.loop(0, n - 1)
+    def _(i):
+        d = dest(i)
+        gather_item(d)
+
         @pl.when(i == 0)
         def _():
             links = has_left.astype(jnp.int32) + has_right.astype(jnp.int32) + 1
@@ -205,6 +208,8 @@
                     @pl.when(ahead <= z)
                     def _():
                         pass_right(z + gap, p)
+
+    gather_item(z)
 
     for p in range(PIECES):
         @pl.when(has_left)

time: 22.5 us -> 22.5 us (level)
  no operation moved by 1% of the time
where the time goes in v4:
time: 22.5 us; the launch traced here: 22.4 us
  Pallas kernels  21.7 us (96%)
  local copies, waits for them, and re-layouts  0.71 us (3%)
    pallas_call x1, Pallas kernels, per_device(): pl.pallas_call(functools.partial(merge_kernel, n), out_shape=jax.ShapeDty...  17.3 us
    pallas_call x1, Pallas kernels, per_device(): pl.pallas_call(functools.partial(angle_kernel, nkern), out_shape=[held((c...  4.31 us
    unnamed x1, local copies, waits for them, and re-layouts  0.71 us

profile of v4, /device:TPU:0, one launch (start us, length us, event | category | flops | bytes accessed | tf_op | source)
XLA Modules:
  0.0 22.4 jit_solution(4978323396156894216)
XLA Ops:
  0.0 4.3 %angle.1 = (f32[64,128,256]{2,1,0:T(8,128)S(1)}, bf16[2048,256]{1,0:T(8,128)(2,1)S(1)}, bf16[2048,256]{1,0:T(8,128)(2,1)S(1)}) custom-call(s32[64]{0:T(128)} %bitcast.8, s32[64]{0:T(128)} %bitcast.9, bf16[128,256]{1,0:T(8,128)(2,1)} %bitcast.7, bf16[8,128,256]{2,1,0:T(8,128)(2,1)} %angle_hbm.1, bf16[8,128,256]{2,1,0:T(8,128)(2,1)} %rng_hbm.1, ...), custom_call_target="tpu_custom_call" | custom-call | tf_op jit(solution)/shard_map/angle/pallas_call | solution.py:264
  4.3 17.3 %merge.1 = f32[2,128,256]{2,1,0:T(8,128)S(1)} custom-call(f32[64,128,256]{2,1,0:T(8,128)S(1)} %get-tuple-element.8.y, bf16[2048,256]{1,0:T(8,128)(2,1)S(1)} %get-tuple-element.9.ghi, bf16[2048,256]{1,0:T(8,128)(2,1)S(1)} %get-tuple-element.10.glo, f32[2,128]{1,0:T(2,128)} %twiddle.1), custom_call_target="tpu_custom_call" | custom-call | tf_op jit(solution)/shard_map/merge/pallas_call | solution.py:291
  21.7 0.7 %copy.9 = f32[1,2,128,256]{3,2,1,0:T(8,128)} copy(f32[1,2,128,256]{3,2,1,0:T(8,128)S(1)} %bitcast.5) | data formatting | bytes 524288
